TPU v7x, 32 devices: a whole 2x2x4 slice. The times are simulated.
32 devices in a mesh: sub: 8 (over z, y), loc: 4 (over x, core).
Axes of the slice: x: 2, y: 2, z: 4, core: 2. Of those that a mesh axis runs over, the one named last changes fastest.
Arguments:
- load_cases: float32 [32, 256, 1024], P(('sub', 'loc')), may hold values from -6 to 6
- schur_matrix: bfloat16 [32, 1024, 1024], P(('sub', 'loc')), as said below
- neumann: bfloat16 [32, 1024, 1024], P(('sub', 'loc')), as said below
- stiffness: float32 [32, 1024], P(('sub', 'loc')), may hold values from 0.1 to 10
- face_map: int32 [32, 2, 256], P(('sub', 'loc')), may hold values from 0 to 255, each once within a row
- coarse_basis: float32 [32, 1024, 16], P(('sub', 'loc')), may hold values from -0.5 to 0.5
- corner_map: int32 [32, 16], P(('sub', 'loc')), may hold values from 0 to 31, as said below
- owner_map: int32 [8, 32], P('sub'), may hold values from 0 to 3, as said below
- level2_inverse: float32 [8, 32, 32], P('sub'), as said below
- level3_map: int32 [8, 32], P('sub'), may hold values from 0 to 63, as said below
- level3_weight: float32 [8, 32], P('sub'), may hold values from 0.5 to 1.5
- level3_inverse: float32 [64, 64], replicated, as said below
Outputs:
- solution: float32 [32, 256, 1024], P(('sub', 'loc'))
- residual: float32 [32, 256, 1024], P(('sub', 'loc'))
Inputs may be any that keep to these rules, and one draw needn't show every extreme that they name: Each face_map[g, i] is a permutation. `corner_map`: within each group every level-2 degree of freedom is named by some entry of its 4 subdomains. `owner_map`: within one group at most 16 level-2 degrees of freedom have the same owner, and some owner has exactly 16. `level3_map`: every level-3 degree of freedom is named. `schur_matrix`: each matrix is symmetric positive definite. `neumann`: each matrix is symmetric positive definite. `level2_inverse`: each matrix is symmetric positive definite. `level3_inverse`: symmetric positive definite.
All inputs are finite; a program needn't handle non-finite values.
Results may differ from a plain program's by a relative error of at most 0.0031.
Values sent between devices are 32-bit elements; how exact they have to be, the bound alone decides.
A program may use at most 64 MiB of HBM per device.

v0:
```python
import jax
import jax.numpy as jnp
from jax import lax
from jax.sharding import PartitionSpec as P

ITERS = 2


highest = lax.Precision.HIGHEST


def padded(cells, sides, width):
    for axis, dim in sides:
        count = lax.axis_size(axis)
        ends = count - 1
        head = lax.slice_in_dim(cells, 0, width, axis=dim)
        tail = lax.slice_in_dim(cells, cells.shape[dim] - width, cells.shape[dim], axis=dim)
        cells = jnp.concatenate(
            [
                lax.ppermute(tail, axis, [(i, (i + 1) % count) for i in range(ends)]),
                cells,
                lax.ppermute(head, axis, [((i + 1) % count, i) for i in range(ends)]),
            ],
            axis=dim,
        )
    return cells


def permute_face(face_values, order_index):
    return jnp.take(face_values, order_index, axis=-1)


def shared_sum(values, face_maps, face_backs):
    face_width = face_maps.shape[-1]
    left_face = values[..., :face_width]
    right_face = values[..., face_width : 2 * face_width]
    top_face = values[..., 2 * face_width : 3 * face_width]
    bottom_face = values[..., 3 * face_width :]
    sideways = jnp.stack([permute_face(left_face, face_backs[0]), right_face])
    across_sub = padded(sideways, (("sub", 0),), 1)
    vertical = jnp.stack([permute_face(top_face, face_backs[1]), bottom_face])
    across_loc = padded(vertical, (("loc", 0),), 1)
    return jnp.concatenate(
        [
            left_face + permute_face(across_sub[0], face_maps[0]),
            right_face + across_sub[3],
            top_face + permute_face(across_loc[0], face_maps[1]),
            bottom_face + across_loc[3],
        ],
        axis=-1,
    )


def global_total(value):
    return lax.psum(value, ("sub", "loc"))


def on_device(
    load_cases,
    schur_matrix,
    neumann,
    stiffness,
    face_map,
    coarse_basis,
    corner_map,
    owner_map,
    level2_inverse,
    level3_map,
    level3_weight,
    level3_inverse,
):
    face_maps = face_map[0]
    face_backs = jnp.argsort(face_maps, axis=-1)
    load_rows = load_cases.shape[1]
    schur_local = schur_matrix[0]
    neumann_local = neumann[0]
    basis = coarse_basis[0]
    corners = corner_map[0]
    owners = owner_map[0]
    inverse_two = level2_inverse[0]
    level3_dofs = level3_map[0]
    level3_scale = level3_weight[0]
    level2_count = inverse_two.shape[-1]
    level3_count = level3_inverse.shape[-1]
    capacity = basis.shape[-1]
    contract_first = (((0,), (1,)), ((), ()))
    combined = shared_sum(
        jnp.concatenate([load_cases[0], stiffness], axis=0), face_maps, face_backs
    )
    right_side = combined[:load_rows]
    weights = stiffness[0] / combined[load_rows]
    corner_onehot = (corners[None, :] == jnp.arange(level2_count, dtype=jnp.int32)[:, None]).astype(
        jnp.float32
    )
    level3_onehot = (
        level3_dofs[None, :] == jnp.arange(level3_count, dtype=jnp.int32)[:, None]
    ).astype(jnp.float32)
    same_flags = owners[:, None] == owners[None, :]
    owner_index = lax.axis_index("loc")

    def precondition(resid_field):
        restricted = weights * resid_field
        local_solve = jnp.dot(
            restricted.astype(jnp.bfloat16), neumann_local, preferred_element_type=jnp.float32
        )
        coarse = lax.dot_general(
            basis, restricted, contract_first, precision=highest, preferred_element_type=jnp.float32
        )
        group_part = jnp.dot(corner_onehot, coarse, precision=highest)
        loc_count = lax.axis_size("loc")
        positions = jnp.arange(level2_count, dtype=jnp.int32)
        earlier = (positions[None, :] < positions[:, None]) & same_flags
        slot_rank = jnp.sum(earlier.astype(jnp.int32), axis=1)
        slot_target = owners * capacity + slot_rank
        placement = (
            jnp.arange(loc_count * capacity, dtype=jnp.int32)[:, None] == slot_target[None, :]
        ).astype(jnp.float32)
        outgoing = jnp.dot(placement, group_part, precision=highest)
        owned_sum = lax.psum_scatter(outgoing, "loc", scatter_dimension=0, tiled=True)
        selected = lax.dynamic_slice_in_dim(placement, owner_index * capacity, capacity, 0)
        owner_block = jnp.dot(
            jnp.dot(selected, inverse_two, precision=highest), selected.T, precision=highest
        )
        owner_update = jnp.dot(owner_block, owned_sum, precision=highest)
        owned_dofs = jnp.dot(selected.T, owned_sum, precision=highest)
        level3_part = jnp.dot(level3_onehot, level3_scale[:, None] * owned_dofs, precision=highest)
        level3_sum = lax.psum(level3_part, ("sub", "loc"))
        level3_update = jnp.dot(level3_inverse, level3_sum, precision=highest)
        back_level3 = level3_scale[:, None] * jnp.dot(
            level3_onehot.T, level3_update, precision=highest
        )
        owner_update = owner_update + jnp.dot(selected, back_level3, precision=highest)
        gathered = lax.all_gather(owner_update, "loc", axis=0, tiled=True)
        level2_update = jnp.dot(placement.T, gathered, precision=highest)
        corner_update = jnp.dot(corner_onehot.T, level2_update, precision=highest)
        fine_update = local_solve + lax.dot_general(
            corner_update,
            basis,
            contract_first,
            precision=highest,
            preferred_element_type=jnp.float32,
        )
        precond = shared_sum(weights * fine_update, face_maps, face_backs)
        product_sum = global_total(jnp.sum(weights * resid_field * precond))
        return (precond, product_sum)

    solution = jnp.zeros_like(right_side)
    residual = right_side
    precond, current = precondition(residual)
    direction = precond
    for iteration in range(ITERS):
        product = jnp.dot(
            direction.astype(jnp.bfloat16), schur_local, preferred_element_type=jnp.float32
        )
        image_field = shared_sum(product, face_maps, face_backs)
        curvature = global_total(jnp.sum(weights * direction * image_field))
        step_size = current / curvature
        solution = solution + step_size * direction
        residual = residual - step_size * image_field
        if iteration + 1 < ITERS:
            precond, following = precondition(residual)
            direction = precond + following / current * direction
            current = following
    return (solution[None], residual[None])


def solution(mesh):
    placed = (
        P(("sub", "loc"), None, None),
        P(("sub", "loc"), None, None),
        P(("sub", "loc"), None, None),
        P(("sub", "loc"), None),
        P(("sub", "loc"), None, None),
        P(("sub", "loc"), None, None),
        P(("sub", "loc"), None),
        P("sub", None),
        P("sub", None, None),
        P("sub", None),
        P("sub", None),
        P(),
    )
    return jax.shard_map(
        on_device,
        mesh=mesh,
        in_specs=placed,
        out_specs=(P(("sub", "loc"), None, None), P(("sub", "loc"), None, None)),
        check_vma=False,
    )
```

profile of v0, /device:TPU:0, one launch (start us, length us, event | category | flops | bytes accessed | tf_op | source)
XLA Modules:
  0.0 658.2 jit_solution(17063242641149399351)
XLA Ops:
  8.4 5.7 collective-permute-start
  18.3 1.3 fusion.62
  22.0 1.7 gather_fusion
  24.8 1.5 bitcast_add_fusion.3
  27.4 1.9 gather_fusion.1
  30.4 1.4 select_bitcast_fusion.1
  35.0 6.8 %collective-permute-done.1 = f32[1,257,256]{2,1,0:T(8,128)S(1)} collective-permute-done((f32[1,257,256]{2,1,0:T(8,128)}, f32[1,257,256]{2,1,0:T(8,128)S(1)}, u32[]{:S(2)}, u32[]{:S(2)}) %collective-permute-start.1) | collective-permute-done | bytes 263200 | tf_op jit(solution)/shard_map/ppermute | solution.py:22
  42.6 1.3 collective-permute-start.2
  47.0 1.9 gather_fusion.2
  48.8 1.8 copy.59
  50.7 1.7 bitcast_add_fusion.1
  53.6 1.7 gather_fusion.3
  58.1 5.8 collective-permute-done.3
  67.1 1.7 fusion.6
  68.8 22.5 %reduce-scatter.3.cloned.1.call-done = f32[16,256]{1,0:T(8,128)} async-done(((f32[64,256]{1,0:T(8,128)}), f32[16,256]{1,0:T(8,128)}) %reduce-scatter.3.cloned.1.call-update) | async-done | bytes 16400 | tf_op jit(solution)/shard_map/reduce_scatter | solution.py:119
  94.0 120.5 %all-reduce.4.cloned.1.call-done = f32[64,256]{1,0:T(8,128)} async-done(((f32[64,256]{1,0:T(8,128)}), f32[64,256]{1,0:T(8,128)}) %all-reduce.4.cloned.1.call-update) | async-done | bytes 65552 | tf_op jit(solution)/shard_map/psum | solution.py:127
  216.1 6.2 all_gather.6
  222.8 2.3 fusion.9
  227.1 1.7 gather_fusion.7
  231.7 1.7 gather_fusion.5
  234.5 2.7 collective-permute-start.4
  237.2 2.7 collective-permute-start.6
  240.6 1.4 collective-permute-start.5
  242.0 1.5 collective-permute-start.7
  245.3 1.7 gather_fusion.4
  247.0 1.8 copy.63
  249.9 1.7 gather_fusion.6
  252.7 1.4 bitcast_add_fusion.19
  259.4 5.0 collective-permute-start.8
  264.4 3.1 collective-permute-start.10
  272.9 1.7 gather_fusion.10
  274.6 1.9 copy.75
  276.5 2.3 collective-permute-done.9
  278.9 1.6 bitcast_add_fusion.15
  281.6 45.6 %all-reduce = (f32[]{:T(128)}, f32[]{:T(128)}) all-reduce(f32[]{:T(128)} %get-tuple-element.7, f32[]{:T(128)} %get-tuple-element.6), channel_id=1, replica_groups=mesh['sub'=8,'loc'=4] {'sub','loc'}, use_global_device_ids=true, to_apply=%region_5.8 | all-reduce | flops 2 | bytes 16 | tf_op jit(solution)/shard_map/psum | solution.py:55
  328.5 1.6 multiply_subtract_fusion
  332.1 1.7 fusion.4
  333.8 17.8 %reduce-scatter.5.cloned.1.call-done = f32[16,256]{1,0:T(8,128)} async-done(((f32[64,256]{1,0:T(8,128)}), f32[16,256]{1,0:T(8,128)}) %reduce-scatter.5.cloned.1.call-update) | async-done | bytes 16400 | tf_op jit(solution)/shard_map/reduce_scatter | solution.py:119
  354.2 121.9 %all-reduce.6.cloned.1.call-done = f32[64,256]{1,0:T(8,128)} async-done(((f32[64,256]{1,0:T(8,128)}), f32[64,256]{1,0:T(8,128)}) %all-reduce.6.cloned.1.call-update) | async-done | bytes 65552 | tf_op jit(solution)/shard_map/psum | solution.py:127
  477.7 6.2 all_gather.7
  484.4 2.3 fusion.8
  489.1 1.7 gather_fusion.15
  493.7 1.7 gather_fusion.13
  496.4 2.7 collective-permute-start.12
  499.1 2.6 collective-permute-start.14
  503.8 1.5 collective-permute-start.15
  507.2 1.7 gather_fusion.12
  508.9 1.8 copy.79
  511.8 1.7 gather_fusion.14
  513.4 1.8 copy.83
  515.3 1.7 bitcast_add_fusion.11
  518.8 47.2 %psum.46 = f32[]{:T(128)} all-reduce(f32[]{:T(128)} %multiply_reduce_fusion.1), channel_id=1, replica_groups=mesh['sub'=8,'loc'=4] {'sub','loc'}, use_global_device_ids=true, to_apply=%region_11.14 | all-reduce | flops 1 | bytes 8 | tf_op jit(solution)/shard_map/psum | solution.py:55
  567.3 2.9 fusion
  572.6 1.7 gather_fusion.19
  577.2 1.7 gather_fusion.17
  580.0 4.4 collective-permute-start.16
  584.4 2.0 collective-permute-start.18
  591.5 1.7 gather_fusion.16
  593.2 1.8 copy.87
  596.1 1.7 gather_fusion.18
  597.7 1.8 copy.91
  599.6 1.8 bitcast_add_fusion.7
  603.4 43.3 %psum.47 = f32[]{:T(128)} all-reduce(f32[]{:T(128)} %multiply_reduce_fusion), channel_id=1, replica_groups=mesh['sub'=8,'loc'=4] {'sub','loc'}, use_global_device_ids=true, to_apply=%region_13.16 | all-reduce | flops 1 | bytes 8 | tf_op jit(solution)/shard_map/psum | solution.py:55
  648.0 2.4 subtract_bitcast_fusion
  (299 shorter events, 87.4 us)
Async XLA Ops:
  7.2 59.9 %copy-start = (bf16[1,1024,1024]{2,1,0:T(8,128)(2,1)S(1)}, bf16[1,1024,1024]{2,1,0:T(8,128)(2,1)}, u32[]{:S(2)}) copy-start(bf16[1,1024,1024]{2,1,0:T(8,128)(2,1)} %param.18) | copy-start | bytes 6291460
  7.2 11.1 %sort.19.cloned.1.call-start = ((), (), s32[]{:S(2)}) async-start(), calls=%async_computation.6 | async-start | bytes 12320 | tf_op jit(solution)/shard_map/jit(argsort)/sort | solution.py:73
  8.4 16.5 %copy-start.1 = (f32[1,256,1024]{2,1,0:T(8,128)S(1)}, f32[1,256,1024]{2,1,0:T(8,128)}, u32[]{:S(2)}) copy-start(f32[1,256,1024]{2,1,0:T(8,128)} %param.16) | copy-start | bytes 3145732
  8.4 16.5 %copy-start.56 = (f32[1,1024]{1,0:T(1,128)S(1)}, f32[1,1024]{1,0:T(1,128)}, u32[]{:S(2)}) copy-start(f32[1,1024]{1,0:T(1,128)} %param.19) | copy-start | bytes 12292
  8.4 12.4 %collective-permute-start = (f32[1,257,256]{2,1,0:T(8,128)S(1)}, f32[1,257,256]{2,1,0:T(8,128)}, u32[]{:S(2)}, u32[]{:S(2)}) collective-permute-start(f32[1,257,256]{2,1,0:T(8,128)S(1)} %fusion.59), channel_id=1, source_target_pairs={{0,4},{4,8},{8,12},{12,16},{16,20},{20,24},{24,28},{1,5},{5,9},{9,... | collective-permute-start | bytes 789512 | tf_op jit(solution)/shard_map/ppermute | solution.py:20
  14.7 76.6 %reduce-scatter.3.cloned.1.call-start = ((), (), s32[]{:S(2)}) async-start(), calls=%async_computation.2 | async-start | bytes 81920 | tf_op jit(solution)/shard_map/reduce_scatter | solution.py:119
  29.3 15.3 %copy-start.79 = (s32[1,256]{1,0:T(1,128)S(1)}, s32[1,256]{1,0:T(1,128)}, u32[]{:S(2)}) copy-start(s32[1,256]{1,0:T(1,128)} %get-tuple-element.49) | copy-start | bytes 3076
  31.8 10.0 %collective-permute-start.1 = (f32[1,257,256]{2,1,0:T(8,128)}, f32[1,257,256]{2,1,0:T(8,128)S(1)}, u32[]{:S(2)}, u32[]{:S(2)}) collective-permute-start(f32[1,257,256]{2,1,0:T(8,128)} %select_bitcast_fusion.1), channel_id=1, source_target_pairs={{4,0},{8,4},{12,8},{16,12},{20,16},{24,20},{28,24},{5,1},{9,5},{13... | collective-permute-start | bytes 789512 | tf_op jit(solution)/shard_map/ppermute | solution.py:22
  42.6 2.5 collective-permute-start.2
  48.8 4.8 copy-start.59
  52.4 14.7 %copy-start.9 = (f32[257,256]{1,0:T(8,128)}, f32[257,256]{1,0:T(8,128)S(1)}, u32[]{:S(2)}) copy-start(f32[257,256]{1,0:T(8,128)S(1)} %get-tuple-element.12) | copy-start | bytes 789508
  52.4 4.2 copy-start.66
  52.4 5.5 copy-start.63
  53.6 11.3 %copy-start.3 = (f32[257,256]{1,0:T(8,128)S(1)}, f32[257,256]{1,0:T(8,128)}, u32[]{:S(2)}) copy-start(f32[257,256]{1,0:T(8,128)} %get-tuple-element.14) | copy-start | bytes 789508
  53.6 11.3 %copy-start.7 = (f32[257,256]{1,0:T(8,128)S(1)}, f32[257,256]{1,0:T(8,128)}, u32[]{:S(2)}) copy-start(f32[257,256]{1,0:T(8,128)} %get-tuple-element.10) | copy-start | bytes 789508
  55.4 9.6 %copy-start.50 = (f32[1,1024,16]{1,2,0:T(8,128)S(1)}, f32[1,1024,16]{1,2,0:T(8,128)}, u32[]{:S(2)}) copy-start(f32[1,1024,16]{1,2,0:T(8,128)} %param.21) | copy-start | bytes 196612
  56.6 9.4 %copy-start.76 = (s32[1,16]{1,0:T(1,128)S(1)}, s32[1,16]{1,0:T(1,128)}, u32[]{:S(2)}) copy-start(s32[1,16]{1,0:T(1,128)} %param.22) | copy-start | bytes 196
  56.6 7.4 %collective-permute-start.3 = (f32[1,257,256]{2,1,0:T(8,128)S(1)}, f32[1,257,256]{2,1,0:T(8,128)S(1)}, u32[]{:S(2)}, u32[]{:S(2)}) collective-permute-start(f32[1,257,256]{2,1,0:T(8,128)S(1)} %select_bitcast_fusion), channel_id=1, source_target_pairs={{1,0},{2,1},{3,2},{5,4},{6,5},{7,6},{9,8},{10,9},{11,10},{13,12},{... | collective-permute-start | bytes 789512 | tf_op jit(solution)/shard_map/ppermute | solution.py:22
  58.1 8.0 %copy-start.71 = (s32[32]{0:T(128)S(1)}, s32[32]{0:T(128)}, u32[]{:S(2)}) copy-start(s32[32]{0:T(128)} %copy-done.70) | copy-start | bytes 388
  64.9 3.9 copy-start.5
  67.0 24.4 %copy-start.80 = (f32[1,32]{1,0:T(1,128)S(1)}, f32[1,32]{1,0:T(1,128)}, u32[]{:S(2)}) copy-start(f32[1,32]{1,0:T(1,128)} %param.26) | copy-start | bytes 388
  67.0 25.3 %copy-start.74 = (s32[1,32]{1,0:T(1,128)S(1)}, s32[1,32]{1,0:T(1,128)}, u32[]{:S(2)}) copy-start(s32[1,32]{1,0:T(1,128)} %param.25) | copy-start | bytes 388
  67.0 147.5 %copy-start.55 = (f32[64,64]{1,0:T(8,128)S(1)}, f32[64,64]{1,0:T(8,128)}, u32[]{:S(2)}) copy-start(f32[64,64]{1,0:T(8,128)} %param.27) | copy-start | bytes 49156
  67.0 147.5 %all-reduce.4.cloned.1.call-start = ((), (), s32[]{:S(2)}) async-start(), calls=%async_computation.3 | async-start | bytes 131072 | tf_op jit(solution)/shard_map/psum | solution.py:127
  93.1 258.5 %reduce-scatter.5.cloned.1.call-start = ((), (), s32[]{:S(2)}) async-start(), calls=%async_computation.4 | async-start | bytes 81920 | tf_op jit(solution)/shard_map/reduce_scatter | solution.py:119
  227.1 4.6 copy-start.58
  229.9 10.0 %copy-start.64 = (pred[256]{0:T(512)(128)(4,1)S(1)}, pred[256]{0:T(512)(128)(4,1)}, u32[]{:S(2)}) copy-start(pred[256]{0:T(512)(128)(4,1)} %compare_and_fusion.2) | copy-start | bytes 772
  234.5 9.0 %collective-permute-start.4 = (f32[1,256,256]{2,1,0:T(8,128)}, f32[1,256,256]{2,1,0:T(8,128)S(1)}, u32[]{:S(2)}, u32[]{:S(2)}) collective-permute-start(f32[1,256,256]{2,1,0:T(8,128)} %get-tuple-element.44), channel_id=1, source_target_pairs={{0,4},{4,8},{8,12},{12,16},{16,20},{20,24},{24,28},{1,5},{5,9},{9,... | collective-permute-start | bytes 786440 | tf_op jit(solution)/shard_map/ppermute | solution.py:20
  237.2 11.6 %collective-permute-start.6 = (f32[1,256,256]{2,1,0:T(8,128)}, f32[1,256,256]{2,1,0:T(8,128)}, u32[]{:S(2)}, u32[]{:S(2)}) collective-permute-start(f32[1,256,256]{2,1,0:T(8,128)} %get-tuple-element.45), channel_id=1, source_target_pairs={{0,1},{1,2},{2,3},{4,5},{5,6},{6,7},{8,9},{9,10},{10,11},{12,13},{... | collective-permute-start | bytes 786440 | tf_op jit(solution)/shard_map/ppermute | solution.py:20
  240.6 9.3 %copy-start.57 = (s32[1024]{0:T(1024)S(1)}, s32[1024]{0:T(1024)}, u32[]{:S(2)}) copy-start(s32[1024]{0:T(1024)} %pad_clamp_fusion.1) | copy-start | bytes 12292
  240.6 12.1 %collective-permute-start.5 = (f32[1,256,256]{2,1,0:T(8,128)}, f32[1,256,256]{2,1,0:T(8,128)}, u32[]{:S(2)}, u32[]{:S(2)}) collective-permute-start(f32[1,256,256]{2,1,0:T(8,128)} %select_bitcast_fusion.9), channel_id=1, source_target_pairs={{4,0},{8,4},{12,8},{16,12},{20,16},{24,20},{28,24},{5,1},{9,5},{13... | collective-permute-start | bytes 786440 | tf_op jit(solution)/shard_map/ppermute | solution.py:22
  242.0 10.7 %collective-permute-start.7 = (f32[1,256,256]{2,1,0:T(8,128)}, f32[1,256,256]{2,1,0:T(8,128)}, u32[]{:S(2)}, u32[]{:S(2)}) collective-permute-start(f32[1,256,256]{2,1,0:T(8,128)} %select_bitcast_fusion.8), channel_id=1, source_target_pairs={{1,0},{2,1},{3,2},{5,4},{6,5},{7,6},{9,8},{10,9},{11,10},{13,12},{... | collective-permute-start | bytes 786440 | tf_op jit(solution)/shard_map/ppermute | solution.py:22
  247.0 5.7 copy-start.60
  247.0 5.7 copy-start.61
  259.4 11.4 %collective-permute-start.8 = (f32[1,256,256]{2,1,0:T(8,128)S(1)}, f32[1,256,256]{2,1,0:T(8,128)S(1)}, u32[]{:S(2)}, u32[]{:S(2)}) collective-permute-start(f32[1,256,256]{2,1,0:T(8,128)S(1)} %get-tuple-element.36), channel_id=1, source_target_pairs={{0,4},{4,8},{8,12},{12,16},{16,20},{20,24},{24,28},{1,5},{5,9},{9,... | collective-permute-start | bytes 786440 | tf_op jit(solution)/shard_map/ppermute | solution.py:20
  264.4 8.4 %collective-permute-start.10 = (f32[1,256,256]{2,1,0:T(8,128)S(1)}, f32[1,256,256]{2,1,0:T(8,128)S(1)}, u32[]{:S(2)}, u32[]{:S(2)}) collective-permute-start(f32[1,256,256]{2,1,0:T(8,128)S(1)} %get-tuple-element.37), channel_id=1, source_target_pairs={{0,1},{1,2},{2,3},{4,5},{5,6},{6,7},{8,9},{9,10},{10,11},{12,13},{... | collective-permute-start | bytes 786440 | tf_op jit(solution)/shard_map/ppermute | solution.py:20
  268.2 10.6 %collective-permute-start.9 = (f32[1,256,256]{2,1,0:T(8,128)}, f32[1,256,256]{2,1,0:T(8,128)}, u32[]{:S(2)}, u32[]{:S(2)}) collective-permute-start(f32[1,256,256]{2,1,0:T(8,128)} %select_bitcast_fusion.7), channel_id=1, source_target_pairs={{4,0},{8,4},{12,8},{16,12},{20,16},{24,20},{28,24},{5,1},{9,5},{13... | collective-permute-start | bytes 786440 | tf_op jit(solution)/shard_map/ppermute | solution.py:22
  269.5 9.3 %collective-permute-start.11 = (f32[1,256,256]{2,1,0:T(8,128)}, f32[1,256,256]{2,1,0:T(8,128)}, u32[]{:S(2)}, u32[]{:S(2)}) collective-permute-start(f32[1,256,256]{2,1,0:T(8,128)} %select_bitcast_fusion.6), channel_id=1, source_target_pairs={{1,0},{2,1},{3,2},{5,4},{6,5},{7,6},{9,8},{10,9},{11,10},{13,12},{... | collective-permute-start | bytes 786440 | tf_op jit(solution)/shard_map/ppermute | solution.py:22
  274.6 6.0 copy-start.4
  274.6 6.0 copy-start.6
  274.6 6.0 copy-start.8
  274.6 6.0 copy-start.10
  276.5 4.1 copy-start.12
  276.5 4.1 copy-start.16
  276.5 4.1 copy-start.20
  276.5 4.1 copy-start.24
  332.0 19.6 %copy-start.81 = (f32[1,32]{1,0:T(1,128)S(1)}, f32[1,32]{1,0:T(1,128)}, u32[]{:S(2)}) copy-start(f32[1,32]{1,0:T(1,128)} %param.26) | copy-start | bytes 388
  332.1 20.5 %copy-start.75 = (s32[1,32]{1,0:T(1,128)S(1)}, s32[1,32]{1,0:T(1,128)}, u32[]{:S(2)}) copy-start(s32[1,32]{1,0:T(1,128)} %param.25) | copy-start | bytes 388
  332.1 151.9 %copy-start.73 = (s32[32]{0:T(128)S(1)}, s32[32]{0:T(128)}, u32[]{:S(2)}) copy-start(s32[32]{0:T(128)} %copy-done.70) | copy-start | bytes 388
  332.1 152.1 %copy-start.78 = (s32[1,16]{1,0:T(1,128)S(1)}, s32[1,16]{1,0:T(1,128)}, u32[]{:S(2)}) copy-start(s32[1,16]{1,0:T(1,128)} %param.22) | copy-start | bytes 196
  332.1 144.0 %all-reduce.6.cloned.1.call-start = ((), (), s32[]{:S(2)}) async-start(), calls=%async_computation.5 | async-start | bytes 131072 | tf_op jit(solution)/shard_map/psum | solution.py:127
  488.0 3.9 copy-start.69
  491.8 9.9 %copy-start.65 = (pred[256]{0:T(512)(128)(4,1)S(1)}, pred[256]{0:T(512)(128)(4,1)}, u32[]{:S(2)}) copy-start(pred[256]{0:T(512)(128)(4,1)} %compare_and_fusion.2) | copy-start | bytes 772
  496.4 9.0 %collective-permute-start.12 = (f32[1,256,256]{2,1,0:T(8,128)}, f32[1,256,256]{2,1,0:T(8,128)S(1)}, u32[]{:S(2)}, u32[]{:S(2)}) collective-permute-start(f32[1,256,256]{2,1,0:T(8,128)} %get-tuple-element.28), channel_id=1, source_target_pairs={{0,4},{4,8},{8,12},{12,16},{16,20},{20,24},{24,28},{1,5},{5,9},{9,... | collective-permute-start | bytes 786440 | tf_op jit(solution)/shard_map/ppermute | solution.py:20
  499.1 11.6 %collective-permute-start.14 = (f32[1,256,256]{2,1,0:T(8,128)}, f32[1,256,256]{2,1,0:T(8,128)}, u32[]{:S(2)}, u32[]{:S(2)}) collective-permute-start(f32[1,256,256]{2,1,0:T(8,128)} %get-tuple-element.29), channel_id=1, source_target_pairs={{0,1},{1,2},{2,3},{4,5},{5,6},{6,7},{8,9},{9,10},{10,11},{12,13},{... | collective-permute-start | bytes 786440 | tf_op jit(solution)/shard_map/ppermute | solution.py:20
  502.5 12.8 %collective-permute-start.13 = (f32[1,256,256]{2,1,0:T(8,128)}, f32[1,256,256]{2,1,0:T(8,128)}, u32[]{:S(2)}, u32[]{:S(2)}) collective-permute-start(f32[1,256,256]{2,1,0:T(8,128)} %select_bitcast_fusion.5), channel_id=1, source_target_pairs={{4,0},{8,4},{12,8},{16,12},{20,16},{24,20},{28,24},{5,1},{9,5},{13... | collective-permute-start | bytes 786440 | tf_op jit(solution)/shard_map/ppermute | solution.py:22
  503.8 11.5 %collective-permute-start.15 = (f32[1,256,256]{2,1,0:T(8,128)}, f32[1,256,256]{2,1,0:T(8,128)}, u32[]{:S(2)}, u32[]{:S(2)}) collective-permute-start(f32[1,256,256]{2,1,0:T(8,128)} %select_bitcast_fusion.4), channel_id=1, source_target_pairs={{1,0},{2,1},{3,2},{5,4},{6,5},{7,6},{9,8},{10,9},{11,10},{13,12},{... | collective-permute-start | bytes 786440 | tf_op jit(solution)/shard_map/ppermute | solution.py:22
  508.9 6.3 copy-start.62
  515.2 52.1 %copy-start.13 = (f32[256,256]{1,0:T(8,128)S(1)}, f32[256,256]{1,0:T(8,128)}, u32[]{:S(2)}) copy-start(f32[256,256]{1,0:T(8,128)} %copy-done.11) | copy-start | bytes 786436
  580.0 9.7 %collective-permute-start.16 = (f32[1,256,256]{2,1,0:T(8,128)}, f32[1,256,256]{2,1,0:T(8,128)S(1)}, u32[]{:S(2)}, u32[]{:S(2)}) collective-permute-start(f32[1,256,256]{2,1,0:T(8,128)} %get-tuple-element.20), channel_id=1, source_target_pairs={{0,4},{4,8},{8,12},{12,16},{16,20},{20,24},{24,28},{1,5},{5,9},{9,... | collective-permute-start | bytes 786440 | tf_op jit(solution)/shard_map/ppermute | solution.py:20
  584.4 10.6 %collective-permute-start.18 = (f32[1,256,256]{2,1,0:T(8,128)}, f32[1,256,256]{2,1,0:T(8,128)}, u32[]{:S(2)}, u32[]{:S(2)}) collective-permute-start(f32[1,256,256]{2,1,0:T(8,128)} %get-tuple-element.21), channel_id=1, source_target_pairs={{0,1},{1,2},{2,3},{4,5},{5,6},{6,7},{8,9},{9,10},{10,11},{12,13},{... | collective-permute-start | bytes 786440 | tf_op jit(solution)/shard_map/ppermute | solution.py:20
  587.1 12.5 %collective-permute-start.17 = (f32[1,256,256]{2,1,0:T(8,128)}, f32[1,256,256]{2,1,0:T(8,128)}, u32[]{:S(2)}, u32[]{:S(2)}) collective-permute-start(f32[1,256,256]{2,1,0:T(8,128)} %select_bitcast_fusion.3), channel_id=1, source_target_pairs={{4,0},{8,4},{12,8},{16,12},{20,16},{24,20},{28,24},{5,1},{9,5},{13... | collective-permute-start | bytes 786440 | tf_op jit(solution)/shard_map/ppermute | solution.py:22
  588.4 11.2 %collective-permute-start.19 = (f32[1,256,256]{2,1,0:T(8,128)}, f32[1,256,256]{2,1,0:T(8,128)}, u32[]{:S(2)}, u32[]{:S(2)}) collective-permute-start(f32[1,256,256]{2,1,0:T(8,128)} %select_bitcast_fusion.2), channel_id=1, source_target_pairs={{1,0},{2,1},{3,2},{5,4},{6,5},{7,6},{9,8},{10,9},{11,10},{13,12},{... | collective-permute-start | bytes 786440 | tf_op jit(solution)/shard_map/ppermute | solution.py:22
  597.7 4.7 copy-start.14
  (44 other events, 76.5 us)
Sparse Core Ops, SparseCore 0:
  14.8 2.5 sort.21.cloned.1.call-done
  67.1 24.1 reduce-scatter.2
  96.9 117.5 all-reduce.3
  332.2 19.3 reduce-scatter.4
  358.5 117.5 all-reduce.5
  (1 shorter events, 0.0 us)
where the time goes:
time: 662 us; the launch traced here: 658 us
  waiting for transfers between devices  298 us (45%)
  blocking collectives  149 us (23%)
  local copies, waits for them, and re-layouts  87.2 us (13%)
  starting transfers between devices  45.7 us (7%)
  other arithmetic  34.8 us (5%)
  matrix products  24.7 us (4%)
  between operations  19.1 us (3%)
    psum x2, waiting for transfers between devices, precondition(): level3_sum = lax.psum(level3_part, ('sub', 'loc'))  242 us
    psum x3, blocking collectives, global_total(): return lax.psum(value, ('sub', 'loc'))  136 us
    gather x40, local copies, waits for them, and re-layouts, permute_face(): return jnp.take(face_values, order_index, axis=-1)  56.6 us
    reduce_scatter x2, waiting for transfers between devices, precondition(): lax.psum_scatter(outgoing, 'loc', scatter_dimension=0, tiled=True)  40.3 us
    ppermute x10, starting transfers between devices, padded(): lax.ppermute(tail, axis, [(i, (i + 1) % count) for i in range(ends)])  32.2 us
    ppermute x10, waiting for transfers between devices, padded(): lax.ppermute(head, axis, [((i + 1) % count, i) for i in range(ends)])  15 us
    ppermute x10, starting transfers between devices, padded(): lax.ppermute(head, axis, [((i + 1) % count, i) for i in range(ends)])  13.4 us
  transfers between devices with their start and end apart: 24, of which 9 were waited for; matrix products, arithmetic and copies ran while one was open for 8% of the time, Pallas kernels for 0%

commit v1 on v0

v1 whole, which is shorter than its diff:
```python
import functools

import jax
import jax.numpy as jnp
from jax import lax
from jax.experimental import pallas as pl
from jax.experimental.pallas import tpu as pltpu
from jax.sharding import PartitionSpec as P

ITERS = 2
EXCHANGES = 1 + 2 * ITERS
MESH = pl.DeviceIdType.MESH
highest = lax.Precision.HIGHEST
f32 = jnp.float32
bf16 = jnp.bfloat16


def dot(a, b, contract=(1, 0), precision=None):
    return lax.dot_general(
        a,
        b,
        (((contract[0],), (contract[1],)), ((), ())),
        precision=precision,
        preferred_element_type=f32,
    )


def tile_sum(block):
    rows, cols = block.shape
    folded = jnp.sum(block.reshape(rows // 8, 8, cols), axis=0)
    total = folded[:, :128]
    for start in range(128, cols, 128):
        total = total + folded[:, start : start + 128]
    return total


def kernel(
    subs,
    locs,
    load_hbm,
    schur_hbm,
    neumann_hbm,
    stiff,
    face_map,
    basis,
    corner,
    owner,
    inverse_two,
    level3_map,
    level3_weight,
    inverse_three,
    solution_out,
    residual_out,
    base,
    received0,
    received,
    schur,
    neumann,
    schur_raw,
    neumann_raw,
    turn,
    weight,
    group_basis,
    level3_scatter,
    r,
    fields,
    rounded,
    direction,
    direction2,
    level2_parts,
    level3_parts,
    level3_rows,
    scalar_loc,
    scalar_sub,
    load_sem,
    face_send,
    face_recv,
    l2_send,
    l2_recv,
    l3_send,
    l3_recv,
    rows_send,
    rows_recv,
    sl_send,
    sl_recv,
    ss_send,
    ss_recv,
):
    me_sub, me_loc = lax.axis_index("sub"), lax.axis_index("loc")
    loads = load_hbm.shape[0]
    width = face_map.shape[-1]
    level2_count = inverse_two.shape[-1]
    level3_count = inverse_three.shape[-1]
    cols = [slice(f * width, (f + 1) * width) for f in range(4)]

    load_copies = [
        pltpu.make_async_copy(load_hbm, base.at[pl.ds(0, loads)], load_sem.at[0]),
        pltpu.make_async_copy(neumann_hbm, neumann_raw, load_sem.at[1]),
        pltpu.make_async_copy(schur_hbm, schur_raw, load_sem.at[2]),
    ]
    for copy in load_copies:
        copy.start()

    barrier = pltpu.get_barrier_semaphore()
    for axis, count, me in (("sub", subs, me_sub), ("loc", locs, me_loc)):
        for d in range(1, count):
            pl.semaphore_signal(
                barrier,
                inc=1,
                device_id={axis: lax.rem(me + d, count)},
                device_id_type=MESH,
            )

    present = (me_sub > 0, me_sub < subs - 1, me_loc > 0, me_loc < locs - 1)
    partner = (
        {"sub": jnp.maximum(me_sub - 1, 0)},
        {"sub": jnp.minimum(me_sub + 1, subs - 1)},
        {"loc": jnp.maximum(me_loc - 1, 0)},
        {"loc": jnp.minimum(me_loc + 1, locs - 1)},
    )
    pending = []

    def face_copy(field, slots, e, f, slot):
        return pltpu.make_async_remote_copy(
            src_ref=field.at[:, cols[f]],
            dst_ref=slots.at[slot],
            send_sem=face_send.at[e, f],
            recv_sem=face_recv.at[e, slot],
            device_id=partner[f],
            device_id_type=MESH,
        )

    def send_face(field, slots, e, f):
        @pl.when(present[f])
        def _():
            face_copy(field, slots, e, f, f ^ 1).start()

        def finish():
            @pl.when(present[f])
            def _():
                face_copy(field, slots, e, f, f ^ 1).wait_send()

        pending.append(finish)

    def receive_face(field, slots, e, f, then):
        @pl.when(present[f])
        def _():
            face_copy(field, slots, e, f, f).wait_recv()
            then()

    def spread(axis, slots, send_sem, recv_sem):
        count, me = (subs, me_sub) if axis == "sub" else (locs, me_loc)

        def make(d, slot):
            peer = lax.rem(me + d, count)
            slot = me if slot is None else peer
            return pltpu.make_async_remote_copy(
                src_ref=slots.at[me],
                dst_ref=slots.at[slot],
                send_sem=send_sem.at[d - 1],
                recv_sem=recv_sem.at[slot],
                device_id={axis: peer},
                device_id_type=MESH,
            )

        for d in range(1, count):
            make(d, None).start()

        def finish():
            for d in range(1, count):
                make(d, None).wait_send()

        pending.append(finish)

        def wait():
            for d in range(1, count):
                make(d, "peer").wait_recv()

        return wait

    def total_of(slots, count):
        total = slots[0]
        for i in range(1, count):
            total = total + slots[i]
        return total

    rows_iota = lax.broadcasted_iota(jnp.int32, (width, width), 0)
    for i in range(2):
        turn[i] = (face_map[i : i + 1, :] == rows_iota).astype(f32)

    load_copies[0].wait()
    base[loads : loads + 8, :] = jnp.broadcast_to(stiff[...], (8, stiff.shape[-1]))
    pl.semaphore_wait(barrier, subs + locs - 2)
    for f in (1, 3):
        send_face(base, received0, 0, f)
    for f in (0, 2):
        base[:, cols[f]] = dot(base[:, cols[f]], turn[f // 2], (1, 1), highest)
        send_face(base, received0, 0, f)

    def reorder(source, target):
        for f in (0, 2):
            one_hot = turn[f // 2].astype(bf16)
            source[cols[f], :] = dot(one_hot, source[cols[f], :]).astype(bf16)
        for f in (0, 2):
            one_hot = turn[f // 2].astype(bf16)
            target[:, cols[f]] = dot(source[:, cols[f]], one_hot, (1, 1)).astype(bf16)
        for f in (1, 3):
            target[:, cols[f]] = source[:, cols[f]]

    load_copies[1].wait()
    reorder(neumann_raw, neumann)
    load_copies[2].wait()
    reorder(schur_raw, schur)

    def named(row, count):
        shape = (count, row.shape[-1])
        return (row == lax.broadcasted_iota(jnp.int32, shape, 0)).astype(f32)

    corner_hot = named(corner[...], level2_count)
    for f in range(4):
        part = dot(corner_hot, basis[cols[f], :], (1, 1), highest)
        if f in (0, 2):
            part = dot(part, turn[f // 2], (1, 1), highest)
        group_basis[:, cols[f]] = part
    level3_scatter[...] = named(level3_map[...], level3_count) * level3_weight[...]
    owner_hot = named(owner[...], max(8, locs))
    masked_two = inverse_two[...] * dot(owner_hot, owner_hot, (0, 0))
    back_three = dot(level3_scatter[...], inverse_three[...], (0, 0), highest)

    for f in (2, 3, 0, 1):
        r[:, cols[f]] = base[:loads, cols[f]]
        weight[:, cols[f]] = base[loads:, cols[f]]

        def add(f=f):
            r[:, cols[f]] += received0[f, :loads]
            weight[:, cols[f]] += received0[f, loads:]

        receive_face(base, received0, 0, f, add)
        weight[:, cols[f]] = base[loads:, cols[f]] / weight[:, cols[f]]
    for f in range(4):
        group_basis[:, cols[f]] *= weight[0:1, cols[f]]

    class Total:
        def __init__(self, i, tile):
            self.i = i
            scalar_loc[i, me_loc] = tile
            self.wait = spread("loc", scalar_loc.at[i], sl_send.at[i], sl_recv.at[i])

        def cross(self):
            self.wait()
            i = self.i
            scalar_sub[i, me_sub] = total_of(scalar_loc.at[i], locs)
            self.wait = spread("sub", scalar_sub.at[i], ss_send.at[i], ss_recv.at[i])

        def value(self):
            self.wait()
            return jnp.sum(total_of(scalar_sub.at[self.i], subs))

    def precondition(k, e):
        z = fields.at[e - 1]
        level2 = jnp.zeros((level2_count, loads), f32)
        for f in range(4):
            rounded[:, cols[f]] = (weight[0:1, cols[f]] * r[:, cols[f]]).astype(bf16)
            level2 += dot(group_basis[:, cols[f]], r[:, cols[f]], (1, 1), highest)
        level2_parts[k, me_loc] = level2
        wait = spread("loc", level2_parts.at[k], l2_send.at[k], l2_recv.at[k])
        for f in (0, 1):
            z[:, cols[f]] = dot(rounded[...], neumann[:, cols[f]]) * weight[0:1, cols[f]]
        wait()
        level2 = total_of(level2_parts.at[k], locs)
        share = level3_count // locs
        mine = level3_scatter[pl.ds(pl.multiple_of(me_loc * share, 8), share), :]
        level3_parts[k, me_sub] = dot(mine, level2, precision=highest)
        wait = spread("sub", level3_parts.at[k], l3_send.at[k], l3_recv.at[k])
        for f in (2, 3):
            z[:, cols[f]] = dot(rounded[...], neumann[:, cols[f]]) * weight[0:1, cols[f]]
        owned = dot(masked_two, level2, precision=highest)
        wait()
        level3_rows[k, me_loc] = total_of(level3_parts.at[k], subs)
        wait = spread("loc", level3_rows.at[k], rows_send.at[k], rows_recv.at[k])
        wait()
        level3 = level3_rows[k].reshape(level3_count, loads)
        update = owned + dot(back_three, level3, precision=highest)
        tile = jnp.zeros((8, 128), f32)
        for f in (0, 1, 2, 3):
            z[:, cols[f]] += dot(update, group_basis[:, cols[f]], (0, 0), highest)
            send_face(z, received.at[e - 1], e, f)
            tile += tile_sum(z[:, cols[f]] * r[:, cols[f]])
        return Total(2 * k, tile)

    def multiply(k, e, source):
        image = fields.at[e - 1]
        for f in range(4):
            rounded[:, cols[f]] = source[:, cols[f]].astype(bf16)
        tile = jnp.zeros((8, 128), f32)
        for f in (0, 1, 2, 3):
            image[:, cols[f]] = dot(rounded[...], schur[:, cols[f]])
            send_face(image, received.at[e - 1], e, f)
            tile += tile_sum(image[:, cols[f]] * source[:, cols[f]])
        return Total(2 * k + 1, tile)

    order = (2, 3, 0, 1)
    previous = None
    current = None
    out_direction = None
    for k in range(ITERS):
        e = 1 + 2 * k
        going = precondition(k, e)
        going.cross()
        z = fields.at[e - 1]
        target = direction if k == 0 else direction2
        for f in order:
            target[:, cols[f]] = z[:, cols[f]]

            def add(f=f):
                target[:, cols[f]] += received[e - 1, f]

            receive_face(z, received.at[e - 1], e, f, add)
        following = going.value()
        if k > 0:
            ratio = following / current
            for f in order:
                target[:, cols[f]] += ratio * direction[:, cols[f]]
        current = following
        e = e + 1
        image = fields.at[e - 1]
        going = multiply(k, e, target)
        going.cross()
        step = current / going.value()
        last = k + 1 == ITERS
        for f in order:
            r[:, cols[f]] -= step * image[:, cols[f]]

            def subtract(f=f):
                r[:, cols[f]] -= step * received[e - 1, f]

            receive_face(image, received.at[e - 1], e, f, subtract)
            if k == 0:
                solution_out[:, cols[f]] = step * target[:, cols[f]]
            else:
                solution_out[:, cols[f]] += step * target[:, cols[f]]
            if last and f in (0, 2):
                one_hot = turn[f // 2]
                solution_out[:, cols[f]] = dot(
                    solution_out[:, cols[f]], one_hot, precision=highest
                )
                residual_out[:, cols[f]] = dot(r[:, cols[f]], one_hot, precision=highest)
            elif last:
                residual_out[:, cols[f]] = r[:, cols[f]]

    for finish in pending:
        finish()


def on_device(mesh, *operands):
    subs, locs = mesh.shape["sub"], mesh.shape["loc"]
    (
        load_cases,
        schur_matrix,
        neumann,
        stiffness,
        face_map,
        basis,
        corner_map,
        owner_map,
        level2_inverse,
        level3_map,
        level3_weight,
        level3_inverse,
    ) = operands
    loads, order = load_cases.shape[1:]
    width = face_map.shape[-1]
    level2_count = level2_inverse.shape[-1]
    level3_count = level3_inverse.shape[-1]
    share = level3_count // locs
    vmem = pl.BlockSpec(memory_space=pltpu.VMEM)
    hbm = pl.BlockSpec(memory_space=pl.ANY)
    dma = pltpu.SemaphoreType.DMA
    field = jax.ShapeDtypeStruct((loads, order), f32)
    extra = EXCHANGES - 1
    totals = 2 * ITERS
    scratch = [
        pltpu.VMEM((loads + 8, order), f32),
        pltpu.VMEM((4, loads + 8, width), f32),
        pltpu.VMEM((extra, 4, loads, width), f32),
        pltpu.VMEM((order, order), bf16),
        pltpu.VMEM((order, order), bf16),
        pltpu.VMEM((order, order), bf16),
        pltpu.VMEM((order, order), bf16),
        pltpu.VMEM((2, width, width), f32),
        pltpu.VMEM((8, order), f32),
        pltpu.VMEM((level2_count, order), f32),
        pltpu.VMEM((level3_count, level2_count), f32),
        pltpu.VMEM((loads, order), f32),
        pltpu.VMEM((extra, loads, order), f32),
        pltpu.VMEM((loads, order), bf16),
        pltpu.VMEM((loads, order), f32),
        pltpu.VMEM((loads, order), f32),
        pltpu.VMEM((ITERS, locs, level2_count, loads), f32),
        pltpu.VMEM((ITERS, subs, share, loads), f32),
        pltpu.VMEM((ITERS, locs, share, loads), f32),
        pltpu.VMEM((totals, locs, 8, 128), f32),
        pltpu.VMEM((totals, subs, 8, 128), f32),
        dma((3,)),
        dma((EXCHANGES, 4)),
        dma((EXCHANGES, 4)),
        dma((ITERS, locs)),
        dma((ITERS, locs)),
        dma((ITERS, subs)),
        dma((ITERS, subs)),
        dma((ITERS, locs)),
        dma((ITERS, locs)),
        dma((totals, locs)),
        dma((totals, locs)),
        dma((totals, subs)),
        dma((totals, subs)),
    ]
    outputs = pl.pallas_call(
        functools.partial(kernel, subs, locs),
        out_shape=(field, field),
        in_specs=[hbm] * 3 + [vmem] * 9,
        out_specs=(vmem, vmem),
        scratch_shapes=scratch,
        compiler_params=pltpu.CompilerParams(
            collective_id=0, has_side_effects=True, vmem_limit_bytes=56 * 1024 * 1024
        ),
    )(
        load_cases[0],
        schur_matrix[0],
        neumann[0],
        stiffness,
        face_map[0],
        basis[0],
        corner_map,
        owner_map,
        level2_inverse[0],
        level3_map,
        level3_weight,
        level3_inverse,
    )
    return tuple(value[None] for value in outputs)


def solution(mesh):
    both = ("sub", "loc")
    cube, flat = P(both, None, None), P(both, None)
    group, group_cube = P("sub", None), P("sub", None, None)
    placed = (cube, cube, cube, flat, cube, cube, flat, group, group_cube, group, group, P())
    return jax.shard_map(
        functools.partial(on_device, mesh),
        mesh=mesh,
        in_specs=placed,
        out_specs=(cube, cube),
        check_vma=False,
    )
```

time: 662 us -> 110 us (0.17)
  waiting for transfers between devices: 298 us -> 0 us
  blocking collectives: 149 us -> 0 us
  Pallas kernels: 0 us -> 104 us
  local copies, waits for them, and re-layouts: 87.2 us -> 5.21 us
  starting transfers between devices: 45.7 us -> 0 us
  other arithmetic: 34.8 us -> 0 us
  matrix products: 24.7 us -> 0 us
  between operations: 19.1 us -> 0.65 us
    psum x2 -> x0, waiting for transfers between devices: 242 us -> none  [precondition(): level3_sum = lax.psum(level3_part, ('sub', 'loc'))]
    psum x3 -> x0, blocking collectives: 136 us -> none  [global_total(): return lax.psum(value, ('sub', 'loc'))]
    pallas_call x0 -> x1, Pallas kernels: none -> 104 us  [on_device(): pl.pallas_call(functools.partial(kernel, subs, locs), out_shape=(field, f...]
    gather x40 -> x0, local copies, waits for them, and re-layouts: 56.6 us -> none  [permute_face(): return jnp.take(face_values, order_index, axis=-1)]
    ppermute x20 -> x0, starting transfers between devices: 45.6 us -> none  [the longest x10 32.2 us: padded(): lax.ppermute(tail, axis, [(i, (i + 1) % count) for i in range(ends)])]
    reduce_scatter x2 -> x0, waiting for transfers between devices: 40.3 us -> none  [precondition(): lax.psum_scatter(outgoing, 'loc', scatter_dimension=0, tiled=True)]
    dot_general x30 -> x0, matrix products: 24.7 us -> none  [the longest x2 4.54 us: precondition(): lax.dot_general(corner_update, basis, contract_first, precision=highest,...]
    ppermute x20 -> x0, waiting for transfers between devices: 15.2 us -> none  [the longest x10 15 us: padded(): lax.ppermute(head, axis, [((i + 1) % count, i) for i in range(ends)])]
  transfers between devices with their start and end apart: 24 -> 0, of which waited for: 9 -> 0; matrix products, arithmetic and copies ran while one was open for 8% -> 0% of each run, Pallas kernels for 0% -> 0%
where the time goes in v1:
time: 110 us
  Pallas kernels  104 us (95%)
  local copies, waits for them, and re-layouts  5.21 us (5%)
    pallas_call x1, Pallas kernels, on_device(): pl.pallas_call(functools.partial(kernel, subs, locs), out_shape=(field, f...  104 us
    unnamed x5, local copies, waits for them, and re-layouts  5.21 us

profile of v1, /device:TPU:0, one launch (start us, length us, event | category | flops | bytes accessed | tf_op | source)
XLA Modules:
  0.0 109.6 jit_solution(13810454275593543352)
XLA Ops:
  0.6 1.8 %copy.14 = f32[1,1024,16]{2,1,0:T(8,128)} copy(f32[1,1024,16]{1,2,0:T(8,128)} %param.17) | data formatting | bytes 131072 | tf_op args[5]
  2.5 103.7 %shard_map.131 = (f32[256,1024]{1,0:T(8,128)}, f32[256,1024]{1,0:T(8,128)}) custom-call(f32[256,1024]{1,0:T(8,128)} %bitcast.13, bf16[1024,1024]{1,0:T(8,128)(2,1)} %bitcast.9, bf16[1024,1024]{1,0:T(8,128)(2,1)} %bitcast.10, f32[1,1024]{1,0:T(1,128)} %stiff.1, s32[2,256]{1,0:T(2,128)} %bitcast.15, f32[1024,16]{1,0:T(8,128)} %bitcast.8, s32[1,16]{1,0:T(1,128)} %corner.1, ...), custom_call_target="tpu_custom_call" | custom-call | tf_op jit(solution)/shard_map/pallas_call | solution.py:418
  106.2 0.0 copy-start
  106.2 2.4 %copy.17 = f32[1,256,1024]{2,1,0:T(8,128)} copy(f32[1,256,1024]{2,1,0:T(8,128)} %bitcast.12) | data formatting | bytes 2097152
  108.6 0.0 copy-done
  108.6 1.0 copy.18
Async XLA Ops:
  106.2 2.4 %copy-start = (f32[256,1024]{1,0:T(8,128)S(1)}, f32[256,1024]{1,0:T(8,128)}, u32[]{:S(2)}) copy-start(f32[256,1024]{1,0:T(8,128)} %get-tuple-element.5) | copy-start | bytes 3145732

commit v2 on v1

v2 whole, which is shorter than its diff:
```python
import functools

import jax
import jax.numpy as jnp
from jax import lax
from jax.experimental import pallas as pl
from jax.experimental.pallas import tpu as pltpu
from jax.sharding import PartitionSpec as P

ITERS = 2
EXCHANGES = 1 + 2 * ITERS
CHUNKS = 2
MESH = pl.DeviceIdType.MESH
highest = lax.Precision.HIGHEST
f32 = jnp.float32
bf16 = jnp.bfloat16


def dot(a, b, contract=(1, 0), precision=None):
    return lax.dot_general(
        a,
        b,
        (((contract[0],), (contract[1],)), ((), ())),
        precision=precision,
        preferred_element_type=f32,
    )


def tile_sum(block):
    rows, cols = block.shape
    folded = jnp.sum(block.reshape(rows // 8, 8, cols), axis=0)
    total = folded[:, :128]
    for start in range(128, cols, 128):
        total = total + folded[:, start : start + 128]
    return total


def kernel(
    subs,
    locs,
    load_hbm,
    schur_hbm,
    neumann_hbm,
    stiff,
    face_map,
    basis,
    corner,
    owner,
    inverse_two,
    level3_map,
    level3_weight,
    inverse_three,
    solution_out,
    residual_out,
    base,
    received0,
    received,
    schur,
    neumann,
    schur_raw,
    neumann_raw,
    turn,
    weight,
    group_basis,
    weighted_basis,
    joint_basis,
    basis_in,
    level3_scatter,
    scatter_in,
    owned_mine,
    owned_in,
    r,
    fields,
    rounded,
    direction,
    direction2,
    solved,
    level2_parts,
    level3_parts,
    level3_rows,
    scalar_loc,
    scalar_sub,
    load_sem,
    out_sem,
    face_send,
    face_recv,
    basis_send,
    basis_recv,
    scatter_send,
    scatter_recv,
    owned_send,
    owned_recv,
    l2_send,
    l2_recv,
    l3_send,
    l3_recv,
    rows_send,
    rows_recv,
    sl_send,
    sl_recv,
    ss_send,
    ss_recv,
):
    me_sub, me_loc = lax.axis_index("sub"), lax.axis_index("loc")
    loads = load_hbm.shape[0]
    width = face_map.shape[-1]
    level2_count = inverse_two.shape[-1]
    level3_count = inverse_three.shape[-1]
    cols = [slice(f * width, (f + 1) * width) for f in range(4)]
    chunk = loads // CHUNKS
    rows = [slice(c * chunk, (c + 1) * chunk) for c in range(CHUNKS)]
    order = (2, 3, 0, 1)

    load_copies = [
        pltpu.make_async_copy(load_hbm, base.at[pl.ds(8, loads)], load_sem.at[0]),
        pltpu.make_async_copy(neumann_hbm, neumann_raw, load_sem.at[1]),
        pltpu.make_async_copy(schur_hbm, schur_raw, load_sem.at[2]),
    ]
    for copy in load_copies:
        copy.start()

    barrier = pltpu.get_barrier_semaphore()
    for axis, count, me in (("sub", subs, me_sub), ("loc", locs, me_loc)):
        for d in range(1, count):
            pl.semaphore_signal(
                barrier,
                inc=1,
                device_id={axis: lax.rem(me + d, count)},
                device_id_type=MESH,
            )

    present = (me_sub > 0, me_sub < subs - 1, me_loc > 0, me_loc < locs - 1)
    partner = (
        {"sub": jnp.maximum(me_sub - 1, 0)},
        {"sub": jnp.minimum(me_sub + 1, subs - 1)},
        {"loc": jnp.maximum(me_loc - 1, 0)},
        {"loc": jnp.minimum(me_loc + 1, locs - 1)},
    )
    pending = []

    class Neighbour:
        def __init__(self, f, source, slot, send_sem, recv_sem):
            self.f = f
            self.make = lambda at: pltpu.make_async_remote_copy(
                src_ref=source,
                dst_ref=slot(at),
                send_sem=send_sem.at[f],
                recv_sem=recv_sem.at[at],
                device_id=partner[f],
                device_id_type=MESH,
            )

        def send(self):
            @pl.when(present[self.f])
            def _():
                self.make(self.f ^ 1).start()

            def finish():
                @pl.when(present[self.f])
                def _():
                    self.make(self.f ^ 1).wait_send()

            pending.append(finish)

        def receive(self, then):
            @pl.when(present[self.f])
            def _():
                self.make(self.f).wait_recv()
                then()

    def face(field, slots, e, c, f, part):
        return Neighbour(
            f,
            field.at[part, cols[f]],
            lambda at: slots.at[at, part],
            face_send.at[e, c],
            face_recv.at[e, c],
        )

    def spread(axis, slots, send_sem, recv_sem):
        count, me = (subs, me_sub) if axis == "sub" else (locs, me_loc)

        def make(d, slot):
            peer = lax.rem(me + d, count)
            slot = me if slot is None else peer
            return pltpu.make_async_remote_copy(
                src_ref=slots.at[me],
                dst_ref=slots.at[slot],
                send_sem=send_sem.at[d - 1],
                recv_sem=recv_sem.at[slot],
                device_id={axis: peer},
                device_id_type=MESH,
            )

        for d in range(1, count):
            make(d, None).start()

        def finish():
            for d in range(1, count):
                make(d, None).wait_send()

        pending.append(finish)

        def wait():
            for d in range(1, count):
                make(d, "peer").wait_recv()

        return wait

    def total_of(slots, count):
        total = slots[0]
        for i in range(1, count):
            total = total + slots[i]
        return total

    rows_iota = lax.broadcasted_iota(jnp.int32, (width, width), 0)
    for i in range(2):
        turn[i] = (face_map[i : i + 1, :] == rows_iota).astype(f32)

    base[0:8, :] = jnp.broadcast_to(stiff[...], (8, stiff.shape[-1]))
    load_copies[0].wait()
    for f in (0, 2):
        base[:, cols[f]] = dot(base[:, cols[f]], turn[f // 2], (1, 1), highest)
    base_parts = [slice(0 if c == 0 else 8 + c * chunk, 8 + (c + 1) * chunk) for c in range(CHUNKS)]
    pl.semaphore_wait(barrier, subs + locs - 2)
    for c in range(CHUNKS):
        for f in range(4):
            face(base, received0, 0, c, f, base_parts[c]).send()

    def named(row, count):
        shape = (count, row.shape[-1])
        return (row == lax.broadcasted_iota(jnp.int32, shape, 0)).astype(f32)

    corner_hot = named(corner[...], level2_count)
    basis_copies = []
    for f in range(4):
        part = dot(corner_hot, basis[:, cols[f]], precision=highest)
        if f in (0, 2):
            part = dot(part, turn[f // 2], (1, 1), highest)
        group_basis[f] = part
        basis_copies.append(
            Neighbour(f, group_basis.at[f], lambda at: basis_in.at[at], basis_send, basis_recv)
        )
        basis_copies[f].send()
    level3_scatter[...] = named(level3_map[...], level3_count) * level3_weight[...]
    scatter_copies = [
        Neighbour(f, level3_scatter, lambda at: scatter_in.at[at], scatter_send, scatter_recv)
        for f in (0, 1)
    ]
    for copy in scatter_copies:
        copy.send()
    owner_hot = named(owner[...], max(8, locs))
    masked_two = inverse_two[...] * dot(owner_hot, owner_hot, (0, 0))

    def reorder(source, target):
        for f in (0, 2):
            one_hot = turn[f // 2].astype(bf16)
            source[cols[f], :] = dot(one_hot, source[cols[f], :]).astype(bf16)
        for f in (0, 2):
            one_hot = turn[f // 2].astype(bf16)
            target[:, cols[f]] = dot(source[:, cols[f]], one_hot, (1, 1)).astype(bf16)
        for f in (1, 3):
            target[:, cols[f]] = source[:, cols[f]]

    load_copies[1].wait()
    reorder(neumann_raw, neumann)
    load_copies[2].wait()
    reorder(schur_raw, schur)

    class Total:
        def __init__(self, i, tile):
            self.i = i
            scalar_loc[i, me_loc] = tile
            self.wait = spread("loc", scalar_loc.at[i], sl_send.at[i], sl_recv.at[i])

        def cross(self):
            self.wait()
            i = self.i
            scalar_sub[i, me_sub] = total_of(scalar_loc.at[i], locs)
            self.wait = spread("sub", scalar_sub.at[i], ss_send.at[i], ss_recv.at[i])

        def value(self):
            self.wait()
            return jnp.sum(total_of(scalar_sub.at[self.i], subs))

    def first_residual(c):
        for f in order:
            r[rows[c], cols[f]] = base[8 + c * chunk : 8 + (c + 1) * chunk, cols[f]]
            if c == 0:
                weight[:, cols[f]] = base[0:8, cols[f]]

            def add(f=f):
                start = 8 + c * chunk
                r[rows[c], cols[f]] += received0[f, start : start + chunk]
                if c == 0:
                    weight[:, cols[f]] += received0[f, 0:8]

            face(base, received0, 0, c, f, base_parts[c]).receive(add)
            if c == 0:
                weight[:, cols[f]] = base[0:8, cols[f]] / weight[:, cols[f]]
                part = group_basis[f] * weight[0:1, cols[f]]
                weighted_basis[:, cols[f]] = part

    def join_bases():
        for f in range(4):
            joint_basis[:, cols[f]] = weighted_basis[:, cols[f]]

            def join(f=f):
                scale = 1.0 - weight[0:1, cols[f]]
                basis_in[f] = basis_in[f] * scale
                if f >= 2:
                    joint_basis[:, cols[f]] += basis_in[f]

            basis_copies[f].receive(join)
        for copy in scatter_copies:
            copy.receive(lambda: None)

    def precondition(k, e, residual_rows, target):
        z = fields.at[e - 1]
        slots = received.at[e - 1]
        tile = jnp.zeros((8, 128), f32)
        for c in range(CHUNKS):
            residual_rows(c)
            level2 = jnp.zeros((level2_count, chunk), f32)
            for f in range(4):
                block = r[rows[c], cols[f]]
                rounded[rows[c], cols[f]] = (weight[0:1, cols[f]] * block).astype(bf16)
                level2 += dot(weighted_basis[:, cols[f]], block, (1, 1), highest)
            level2_parts[k, me_loc, :, rows[c]] = level2
            if c == CHUNKS - 1:
                wait = spread("loc", level2_parts.at[k], l2_send.at[k], l2_recv.at[k])
            for f in range(4):
                part = dot(rounded[rows[c], :], neumann[:, cols[f]]) * weight[0:1, cols[f]]
                z[rows[c], cols[f]] = part
                face(z, slots, e, c, f, rows[c]).send()
                tile += tile_sum(part * r[rows[c], cols[f]])
        wait()
        level2 = total_of(level2_parts.at[k], locs)
        share = level3_count // locs
        mine = level3_scatter[pl.ds(pl.multiple_of(me_loc * share, 8), share), :]
        level3_parts[k, me_sub] = dot(mine, level2, precision=highest)
        wait = spread("sub", level3_parts.at[k], l3_send.at[k], l3_recv.at[k])
        owned = dot(masked_two, level2, precision=highest)
        owned_mine[k] = owned
        owned_copies = [
            Neighbour(
                f,
                owned_mine.at[k],
                lambda at: owned_in.at[k, at],
                owned_send.at[k],
                owned_recv.at[k],
            )
            for f in (0, 1)
        ]
        for copy in owned_copies:
            copy.send()
        going = Total(2 * k, tile + tile_sum(owned * level2_parts[k, me_loc]))
        if k == 0:
            join_bases()
        wait()
        level3_rows[k, me_loc] = total_of(level3_parts.at[k], subs)
        wait = spread("loc", level3_rows.at[k], rows_send.at[k], rows_recv.at[k])
        going.cross()
        wait()
        level3 = level3_rows[k].reshape(level3_count, loads)
        level3_update = dot(inverse_three[...], level3, precision=highest)
        level3_inner = jnp.sum(level3 * level3_update)
        owned_mine_update = owned + dot(level3_scatter[...], level3_update, (0, 0), highest)
        for f in order:
            target[:, cols[f]] = z[:, cols[f]] + dot(
                owned_mine_update, joint_basis[:, cols[f]], (0, 0), highest
            )
        for f in (0, 1):

            def beside(f=f):
                update = owned_in[k, f] + dot(scatter_in[f], level3_update, (0, 0), highest)
                target[:, cols[f]] += dot(update, basis_in[f], (0, 0), highest)

            owned_copies[f].receive(beside)
        return going.value() + level3_inner

    def take_direction(c, e, target):
        for f in order:

            def add(f=f):
                target[rows[c], cols[f]] += received[e - 1, f, rows[c]]

            z = fields.at[e - 1]
            face(z, received.at[e - 1], e, c, f, rows[c]).receive(add)

    current = None
    residual_rows = first_residual
    out_copies = []
    for k in range(ITERS):
        e = 1 + 2 * k
        target = direction if k == 0 else direction2
        following = precondition(k, e, residual_rows, target)
        if k > 0:
            ratio = following / current
            for f in order:
                target[:, cols[f]] += ratio * direction[:, cols[f]]
        current = following
        image = fields.at[e]
        tile = jnp.zeros((8, 128), f32)
        for c in range(CHUNKS):
            take_direction(c, e, target)
            for f in range(4):
                rounded[rows[c], cols[f]] = target[rows[c], cols[f]].astype(bf16)
            for f in range(4):
                part = dot(rounded[rows[c], :], schur[:, cols[f]])
                image[rows[c], cols[f]] = part
                face(image, received.at[e], e + 1, c, f, rows[c]).send()
                tile += tile_sum(part * target[rows[c], cols[f]])
        going = Total(2 * k + 1, tile)
        going.cross()
        step = current / going.value()
        last = k + 1 == ITERS
        for f in order:
            part = step * target[:, cols[f]]
            if k > 0:
                part += solved[:, cols[f]]
            if last and f in (0, 2):
                part = dot(part, turn[f // 2], precision=highest)
            solved[:, cols[f]] = part
        if last:
            out_copies.append(pltpu.make_async_copy(solved, solution_out, out_sem.at[0]))
            out_copies[-1].start()

        def residual_rows(c, image=image, step=step, e=e):
            for f in order:
                r[rows[c], cols[f]] -= step * image[rows[c], cols[f]]

                def subtract(f=f):
                    r[rows[c], cols[f]] -= step * received[e, f, rows[c]]

                face(image, received.at[e], e + 1, c, f, rows[c]).receive(subtract)

    for c in range(CHUNKS):
        residual_rows(c)
        for f in (0, 2):
            r[rows[c], cols[f]] = dot(r[rows[c], cols[f]], turn[f // 2], precision=highest)
        out_copies.append(
            pltpu.make_async_copy(r.at[rows[c]], residual_out.at[rows[c]], out_sem.at[1 + c])
        )
        out_copies[-1].start()

    for finish in pending:
        finish()
    for copy in out_copies:
        copy.wait()


def on_device(mesh, *operands):
    subs, locs = mesh.shape["sub"], mesh.shape["loc"]
    (
        load_cases,
        schur_matrix,
        neumann,
        stiffness,
        face_map,
        basis,
        corner_map,
        owner_map,
        level2_inverse,
        level3_map,
        level3_weight,
        level3_inverse,
    ) = operands
    loads, order = load_cases.shape[1:]
    width = face_map.shape[-1]
    level2_count = level2_inverse.shape[-1]
    level3_count = level3_inverse.shape[-1]
    share = level3_count // locs
    vmem = pl.BlockSpec(memory_space=pltpu.VMEM)
    hbm = pl.BlockSpec(memory_space=pl.ANY)
    dma = pltpu.SemaphoreType.DMA
    field = jax.ShapeDtypeStruct((loads, order), f32)
    extra = EXCHANGES - 1
    totals = 2 * ITERS
    scratch = [
        pltpu.VMEM((loads + 8, order), f32),
        pltpu.VMEM((4, loads + 8, width), f32),
        pltpu.VMEM((extra, 4, loads, width), f32),
        pltpu.VMEM((order, order), bf16),
        pltpu.VMEM((order, order), bf16),
        pltpu.VMEM((order, order), bf16),
        pltpu.VMEM((order, order), bf16),
        pltpu.VMEM((2, width, width), f32),
        pltpu.VMEM((8, order), f32),
        pltpu.VMEM((4, level2_count, width), f32),
        pltpu.VMEM((level2_count, order), f32),
        pltpu.VMEM((level2_count, order), f32),
        pltpu.VMEM((4, level2_count, width), f32),
        pltpu.VMEM((level3_count, level2_count), f32),
        pltpu.VMEM((2, level3_count, level2_count), f32),
        pltpu.VMEM((ITERS, level2_count, loads), f32),
        pltpu.VMEM((ITERS, 2, level2_count, loads), f32),
        pltpu.VMEM((loads, order), f32),
        pltpu.VMEM((extra, loads, order), f32),
        pltpu.VMEM((loads, order), bf16),
        pltpu.VMEM((loads, order), f32),
        pltpu.VMEM((loads, order), f32),
        pltpu.VMEM((loads, order), f32),
        pltpu.VMEM((ITERS, locs, level2_count, loads), f32),
        pltpu.VMEM((ITERS, subs, share, loads), f32),
        pltpu.VMEM((ITERS, locs, share, loads), f32),
        pltpu.VMEM((totals, locs, 8, 128), f32),
        pltpu.VMEM((totals, subs, 8, 128), f32),
        dma((3,)),
        dma((1 + CHUNKS,)),
        dma((EXCHANGES, CHUNKS, 4)),
        dma((EXCHANGES, CHUNKS, 4)),
        dma((4,)),
        dma((4,)),
        dma((2,)),
        dma((2,)),
        dma((ITERS, 2)),
        dma((ITERS, 2)),
        dma((ITERS, locs)),
        dma((ITERS, locs)),
        dma((ITERS, subs)),
        dma((ITERS, subs)),
        dma((ITERS, locs)),
        dma((ITERS, locs)),
        dma((totals, locs)),
        dma((totals, locs)),
        dma((totals, subs)),
        dma((totals, subs)),
    ]
    outputs = pl.pallas_call(
        functools.partial(kernel, subs, locs),
        out_shape=(field, field),
        in_specs=[hbm] * 3 + [vmem] * 9,
        out_specs=(hbm, hbm),
        scratch_shapes=scratch,
        compiler_params=pltpu.CompilerParams(
            collective_id=0, has_side_effects=True, vmem_limit_bytes=56 * 1024 * 1024
        ),
    )(
        load_cases[0],
        schur_matrix[0],
        neumann[0],
        stiffness,
        face_map[0],
        basis[0].T,
        corner_map,
        owner_map,
        level2_inverse[0],
        level3_map,
        level3_weight,
        level3_inverse,
    )
    return tuple(value[None] for value in outputs)


def solution(mesh):
    both = ("sub", "loc")
    cube, flat = P(both, None, None), P(both, None)
    group, group_cube = P("sub", None), P("sub", None, None)
    placed = (cube, cube, cube, flat, cube, cube, flat, group, group_cube, group, group, P())
    return jax.shard_map(
        functools.partial(on_device, mesh),
        mesh=mesh,
        in_specs=placed,
        out_specs=(cube, cube),
        check_vma=False,
    )
```

time: 110 us -> 99.3 us (0.903); the launches traced: 110 us -> 97.6 us
  Pallas kernels: 104 us -> 93.6 us
  local copies, waits for them, and re-layouts: 5.21 us -> 3.37 us
    pallas_call x1, Pallas kernels: 104 us -> 93.6 us  [on_device(): pl.pallas_call(functools.partial(kernel, subs, locs), out_shape=(field, f...]
    unnamed x5 -> x4, local copies, waits for them, and re-layouts: 5.21 us -> 3.37 us
where the time goes in v2:
time: 99.3 us; the launch traced here: 97.6 us
  Pallas kernels  93.6 us (94%)
  local copies, waits for them, and re-layouts  3.37 us (3%)
    pallas_call x1, Pallas kernels, on_device(): pl.pallas_call(functools.partial(kernel, subs, locs), out_shape=(field, f...  93.6 us
    unnamed x4, local copies, waits for them, and re-layouts  3.37 us

profile of v2, /device:TPU:0, one launch (start us, length us, event | category | flops | bytes accessed | tf_op | source)
XLA Modules:
  0.0 97.6 jit_solution(10375171248801621059)
XLA Ops:
  0.6 93.6 %shard_map.131 = (f32[256,1024]{1,0:T(8,128)}, f32[256,1024]{1,0:T(8,128)}) custom-call(f32[256,1024]{1,0:T(8,128)} %bitcast.14, bf16[1024,1024]{1,0:T(8,128)(2,1)} %bitcast.10, bf16[1024,1024]{1,0:T(8,128)(2,1)} %bitcast.11, f32[1,1024]{1,0:T(1,128)} %stiff.1, s32[2,256]{1,0:T(2,128)} %bitcast.17, f32[16,1024]{1,0:T(8,128)} %bitcast.15, s32[1,16]{1,0:T(1,128)} %corner.1, ...), custom_call_target="tpu_custom_call" | custom-call | tf_op jit(solution)/shard_map/pallas_call | solution.py:530
  94.2 0.0 copy-start
  94.2 2.4 %copy.16 = f32[1,256,1024]{2,1,0:T(8,128)} copy(f32[1,256,1024]{2,1,0:T(8,128)} %bitcast.13) | data formatting | bytes 2097152
  96.6 0.0 copy-done
  96.6 1.0 copy.17
Async XLA Ops:
  94.2 2.4 %copy-start = (f32[256,1024]{1,0:T(8,128)S(1)}, f32[256,1024]{1,0:T(8,128)}, u32[]{:S(2)}) copy-start(f32[256,1024]{1,0:T(8,128)} %get-tuple-element.5) | copy-start | bytes 3145732

commit v3 on v2

--- a/solution.py
+++ b/solution.py
@@ -69,6 +69,11 @@
     scatter_in,
     owned_mine,
     owned_in,
+    beside_mine,
+    beside_in,
+    level2_kept,
+    owned_kept,
+    level3_kept,
     r,
     fields,
     rounded,
@@ -90,6 +95,8 @@
     scatter_recv,
     owned_send,
     owned_recv,
+    beside_send,
+    beside_recv,
     l2_send,
     l2_recv,
     l3_send,
@@ -223,9 +230,6 @@
         base[:, cols[f]] = dot(base[:, cols[f]], turn[f // 2], (1, 1), highest)
     base_parts = [slice(0 if c == 0 else 8 + c * chunk, 8 + (c + 1) * chunk) for c in range(CHUNKS)]
     pl.semaphore_wait(barrier, subs + locs - 2)
-    for c in range(CHUNKS):
-        for f in range(4):
-            face(base, received0, 0, c, f, base_parts[c]).send()
 
     def named(row, count):
         shape = (count, row.shape[-1])
@@ -249,6 +253,9 @@
     ]
     for copy in scatter_copies:
         copy.send()
+    for c in range(CHUNKS):
+        for f in range(4):
+            face(base, received0, 0, c, f, base_parts[c]).send()
     owner_hot = named(owner[...], max(8, locs))
     masked_two = inverse_two[...] * dot(owner_hot, owner_hot, (0, 0))
 
@@ -315,68 +322,130 @@
         for copy in scatter_copies:
             copy.receive(lambda: None)
 
-    def precondition(k, e, residual_rows, target):
+    share = level3_count // locs
+
+    class Coarse:
+        def __init__(self, k, block):
+            part = jnp.zeros((level2_count, loads), f32)
+            for f in range(4):
+                part += dot(joint_basis[:, cols[f]], block(f), (1, 1), highest)
+            level2_parts[k, me_loc] = part
+            beside = []
+            for f in (0, 1):
+
+                @pl.when(present[f])
+                def _(f=f):
+                    beside_mine[k, f] = dot(basis_in[f], block(f), (1, 1), highest)
+
+                beside.append(
+                    Neighbour(
+                        f,
+                        beside_mine.at[k, f],
+                        lambda at: beside_in.at[k, at],
+                        beside_send.at[k],
+                        beside_recv.at[k],
+                    )
+                )
+                beside[f].send()
+            self.k, self.beside = k, beside
+
+        def group(self):
+            k = self.k
+            for f in (0, 1):
+
+                def add(f=f):
+                    level2_parts[k, me_loc] += beside_in[k, f]
+
+                self.beside[f].receive(add)
+            self.wait = spread("loc", level2_parts.at[k], l2_send.at[k], l2_recv.at[k])
+
+        def cross(self):
+            k = self.k
+            self.wait()
+            self.level2 = total_of(level2_parts.at[k], locs)
+            mine = level3_scatter[pl.ds(pl.multiple_of(me_loc * share, 8), share), :]
+            level3_parts[k, me_sub] = dot(mine, self.level2, precision=highest)
+            self.wait = spread("sub", level3_parts.at[k], l3_send.at[k], l3_recv.at[k])
+            self.owned = dot(masked_two, self.level2, precision=highest)
+            owned_mine[k] = self.owned
+            self.copies = [
+                Neighbour(
+                    f,
+                    owned_mine.at[k],
+                    lambda at: owned_in.at[k, at],
+                    owned_send.at[k],
+                    owned_recv.at[k],
+                )
+                for f in (0, 1)
+            ]
+            for copy in self.copies:
+                copy.send()
+
+        def gather(self):
+            k = self.k
+            self.wait()
+            level3_rows[k, me_loc] = total_of(level3_parts.at[k], subs)
+            self.wait = spread("loc", level3_rows.at[k], rows_send.at[k], rows_recv.at[k])
+
+        def finish(self):
+            self.wait()
+            self.level3 = level3_rows[self.k].reshape(level3_count, loads)
+
+    coarse = []
+
+    def precondition(k, e, residual_rows, target, step):
         z = fields.at[e - 1]
         slots = received.at[e - 1]
         tile = jnp.zeros((8, 128), f32)
         for c in range(CHUNKS):
             residual_rows(c)
-            level2 = jnp.zeros((level2_count, chunk), f32)
             for f in range(4):
                 block = r[rows[c], cols[f]]
                 rounded[rows[c], cols[f]] = (weight[0:1, cols[f]] * block).astype(bf16)
-                level2 += dot(weighted_basis[:, cols[f]], block, (1, 1), highest)
-            level2_parts[k, me_loc, :, rows[c]] = level2
-            if c == CHUNKS - 1:
-                wait = spread("loc", level2_parts.at[k], l2_send.at[k], l2_recv.at[k])
+            if k == 0 and c == 0:
+                join_bases()
+                coarse.append(Coarse(0, lambda f: base[8:, cols[f]]))
             for f in range(4):
                 part = dot(rounded[rows[c], :], neumann[:, cols[f]]) * weight[0:1, cols[f]]
                 z[rows[c], cols[f]] = part
                 face(z, slots, e, c, f, rows[c]).send()
                 tile += tile_sum(part * r[rows[c], cols[f]])
-        wait()
-        level2 = total_of(level2_parts.at[k], locs)
-        share = level3_count // locs
-        mine = level3_scatter[pl.ds(pl.multiple_of(me_loc * share, 8), share), :]
-        level3_parts[k, me_sub] = dot(mine, level2, precision=highest)
-        wait = spread("sub", level3_parts.at[k], l3_send.at[k], l3_recv.at[k])
-        owned = dot(masked_two, level2, precision=highest)
-        owned_mine[k] = owned
-        owned_copies = [
-            Neighbour(
-                f,
-                owned_mine.at[k],
-                lambda at: owned_in.at[k, at],
-                owned_send.at[k],
-                owned_recv.at[k],
-            )
-            for f in (0, 1)
-        ]
-        for copy in owned_copies:
-            copy.send()
-        going = Total(2 * k, tile + tile_sum(owned * level2_parts[k, me_loc]))
-        if k == 0:
-            join_bases()
-        wait()
-        level3_rows[k, me_loc] = total_of(level3_parts.at[k], subs)
-        wait = spread("loc", level3_rows.at[k], rows_send.at[k], rows_recv.at[k])
+            if k == 0 and c == 0:
+                coarse[0].group()
+                coarse[0].cross()
+        last = coarse[-1]
+        last.gather()
+        level2, owned = last.level2, last.owned
+        if k > 0:
+            level2 = level2_kept[...] - step * level2
+            owned = owned_kept[...] - step * owned
+        level2_kept[...] = level2
+        owned_kept[...] = owned
+        going = Total(2 * k, tile + tile_sum(owned * level2) * (1.0 / locs))
+        last.finish()
+        level3 = last.level3
+        if k > 0:
+            level3 = level3_kept[...] - step * level3
+        level3_kept[...] = level3
         going.cross()
-        wait()
-        level3 = level3_rows[k].reshape(level3_count, loads)
         level3_update = dot(inverse_three[...], level3, precision=highest)
         level3_inner = jnp.sum(level3 * level3_update)
-        owned_mine_update = owned + dot(level3_scatter[...], level3_update, (0, 0), highest)
+        update = owned + dot(level3_scatter[...], level3_update, (0, 0), highest)
         for f in order:
             target[:, cols[f]] = z[:, cols[f]] + dot(
-                owned_mine_update, joint_basis[:, cols[f]], (0, 0), highest
+                update, joint_basis[:, cols[f]], (0, 0), highest
             )
         for f in (0, 1):
 
             def beside(f=f):
-                update = owned_in[k, f] + dot(scatter_in[f], level3_update, (0, 0), highest)
-                target[:, cols[f]] += dot(update, basis_in[f], (0, 0), highest)
-
-            owned_copies[f].receive(beside)
+                theirs = owned_in[k, f]
+                if k > 0:
+                    theirs = owned_in[k - 1, f] - step * theirs
+                    owned_in[k, f] = theirs
+                theirs += dot(scatter_in[f], level3_update, (0, 0), highest)
+                target[:, cols[f]] += dot(theirs, basis_in[f], (0, 0), highest)
+
+            last.copies[f].receive(beside)
         return going.value() + level3_inner
 
     def take_direction(c, e, target):
@@ -389,12 +458,13 @@
             face(z, received.at[e - 1], e, c, f, rows[c]).receive(add)
 
     current = None
+    step = None
     residual_rows = first_residual
     out_copies = []
     for k in range(ITERS):
         e = 1 + 2 * k
         target = direction if k == 0 else direction2
-        following = precondition(k, e, residual_rows, target)
+        following = precondition(k, e, residual_rows, target, step)
         if k > 0:
             ratio = following / current
             for f in order:
@@ -412,9 +482,14 @@
                 face(image, received.at[e], e + 1, c, f, rows[c]).send()
                 tile += tile_sum(part * target[rows[c], cols[f]])
         going = Total(2 * k + 1, tile)
+        last = k + 1 == ITERS
+        if not last:
+            coarse.append(Coarse(k + 1, lambda f, image=image: image[:, cols[f]]))
         going.cross()
+        if not last:
+            coarse[-1].group()
+            coarse[-1].cross()
         step = current / going.value()
-        last = k + 1 == ITERS
         for f in order:
             part = step * target[:, cols[f]]
             if k > 0:
@@ -495,6 +570,11 @@
         pltpu.VMEM((2, level3_count, level2_count), f32),
         pltpu.VMEM((ITERS, level2_count, loads), f32),
         pltpu.VMEM((ITERS, 2, level2_count, loads), f32),
+        pltpu.VMEM((ITERS, 2, level2_count, loads), f32),
+        pltpu.VMEM((ITERS, 2, level2_count, loads), f32),
+        pltpu.VMEM((level2_count, loads), f32),
+        pltpu.VMEM((level2_count, loads), f32),
+        pltpu.VMEM((level3_count, loads), f32),
         pltpu.VMEM((loads, order), f32),
         pltpu.VMEM((extra, loads, order), f32),
         pltpu.VMEM((loads, order), bf16),
@@ -514,6 +594,8 @@
         dma((4,)),
         dma((2,)),
         dma((2,)),
+        dma((ITERS, 2)),
+        dma((ITERS, 2)),
         dma((ITERS, 2)),
         dma((ITERS, 2)),
         dma((ITERS, locs)),

time: 99.3 us -> 105 us (1.057); the launches traced: 97.6 us -> 105 us
  Pallas kernels: 93.6 us -> 101 us
    pallas_call x1, Pallas kernels: 93.6 us -> 101 us  [on_device(): pl.pallas_call(functools.partial(kernel, subs, locs), out_shape=(field, f...]
where the time goes in v3:
time: 105 us
  Pallas kernels  101 us (96%)
  local copies, waits for them, and re-layouts  3.37 us (3%)
    pallas_call x1, Pallas kernels, on_device(): pl.pallas_call(functools.partial(kernel, subs, locs), out_shape=(field, f...  101 us
    unnamed x4, local copies, waits for them, and re-layouts  3.37 us

profile of v3, /device:TPU:0, one launch (start us, length us, event | category | flops | bytes accessed | tf_op | source)
XLA Modules:
  0.0 105.0 jit_solution(4986684503298399663)
XLA Ops:
  0.6 100.9 %shard_map.131 = (f32[256,1024]{1,0:T(8,128)}, f32[256,1024]{1,0:T(8,128)}) custom-call(f32[256,1024]{1,0:T(8,128)} %bitcast.14, bf16[1024,1024]{1,0:T(8,128)(2,1)} %bitcast.10, bf16[1024,1024]{1,0:T(8,128)(2,1)} %bitcast.11, f32[1,1024]{1,0:T(1,128)} %stiff.1, s32[2,256]{1,0:T(2,128)} %bitcast.17, f32[16,1024]{1,0:T(8,128)} %bitcast.15, s32[1,16]{1,0:T(1,128)} %corner.1, ...), custom_call_target="tpu_custom_call" | custom-call | tf_op jit(solution)/shard_map/pallas_call | solution.py:612
  101.6 0.0 copy-start
  101.6 2.4 %copy.16 = f32[1,256,1024]{2,1,0:T(8,128)} copy(f32[1,256,1024]{2,1,0:T(8,128)} %bitcast.13) | data formatting | bytes 2097152
  104.0 0.0 copy-done
  104.0 1.0 copy.17
Async XLA Ops:
  101.6 2.4 %copy-start = (f32[256,1024]{1,0:T(8,128)S(1)}, f32[256,1024]{1,0:T(8,128)}, u32[]{:S(2)}) copy-start(f32[256,1024]{1,0:T(8,128)} %get-tuple-element.5) | copy-start | bytes 3145732

commit v4 on v3

--- a/solution.py
+++ b/solution.py
@@ -412,7 +412,8 @@
                 tile += tile_sum(part * r[rows[c], cols[f]])
             if k == 0 and c == 0:
                 coarse[0].group()
-                coarse[0].cross()
+            if c == (CHUNKS - 1 if k == 0 else 0):
+                coarse[-1].cross()
         last = coarse[-1]
         last.gather()
         level2, owned = last.level2, last.owned
@@ -488,7 +489,6 @@
         going.cross()
         if not last:
             coarse[-1].group()
-            coarse[-1].cross()
         step = current / going.value()
         for f in order:
             part = step * target[:, cols[f]]

time: 105 us -> 101 us (0.962)
  Pallas kernels: 101 us -> 97.3 us
    pallas_call x1, Pallas kernels: 101 us -> 97.3 us  [on_device(): pl.pallas_call(functools.partial(kernel, subs, locs), out_shape=(field, f...]
where the time goes in v4:
time: 101 us
  Pallas kernels  97.3 us (96%)
  local copies, waits for them, and re-layouts  3.37 us (3%)
    pallas_call x1, Pallas kernels, on_device(): pl.pallas_call(functools.partial(kernel, subs, locs), out_shape=(field, f...  97.3 us
    unnamed x4, local copies, waits for them, and re-layouts  3.37 us

profile of v4, /device:TPU:0, one launch (start us, length us, event | category | flops | bytes accessed | tf_op | source)
XLA Modules:
  0.0 101.3 jit_solution(14514841066755976251)
XLA Ops:
  0.6 97.3 %shard_map.131 = (f32[256,1024]{1,0:T(8,128)}, f32[256,1024]{1,0:T(8,128)}) custom-call(f32[256,1024]{1,0:T(8,128)} %bitcast.14, bf16[1024,1024]{1,0:T(8,128)(2,1)} %bitcast.10, bf16[1024,1024]{1,0:T(8,128)(2,1)} %bitcast.11, f32[1,1024]{1,0:T(1,128)} %stiff.1, s32[2,256]{1,0:T(2,128)} %bitcast.17, f32[16,1024]{1,0:T(8,128)} %bitcast.15, s32[1,16]{1,0:T(1,128)} %corner.1, ...), custom_call_target="tpu_custom_call" | custom-call | tf_op jit(solution)/shard_map/pallas_call | solution.py:612
  97.9 0.0 copy-start
  97.9 2.4 %copy.16 = f32[1,256,1024]{2,1,0:T(8,128)} copy(f32[1,256,1024]{2,1,0:T(8,128)} %bitcast.13) | data formatting | bytes 2097152
  100.3 0.0 copy-done
  100.3 1.0 copy.17
Async XLA Ops:
  97.9 2.4 %copy-start = (f32[256,1024]{1,0:T(8,128)S(1)}, f32[256,1024]{1,0:T(8,128)}, u32[]{:S(2)}) copy-start(f32[256,1024]{1,0:T(8,128)} %get-tuple-element.5) | copy-start | bytes 3145732
